TPU v7x, 32 devices: a whole 2x2x4 slice. The times are simulated.
32 devices in a mesh: shots: 2 (over x), gx: 16 (over z, y, core).
Axes of the slice: x: 2, y: 2, z: 4, core: 2. Of those that a mesh axis runs over, the one named last changes fastest.
Arguments:
- courant_sq: float32 [128, 128, 128], P('gx'), may hold values from 0.03 to 0.2
- wave_prev: float32 [256, 128, 128], P(('shots', 'gx')), parts along dimension 0, may hold values from -6 to 6
- wave_now: float32 [256, 128, 128], P(('shots', 'gx')), parts along dimension 0, may hold values from -6 to 6
- adj_late: float32 [256, 128, 128], P(('shots', 'gx')), parts along dimension 0, may hold values from -6 to 6
- adj_last: float32 [256, 128, 128], P(('shots', 'gx')), parts along dimension 0, may hold values from -6 to 6
- wavelet: float32 [24], P('shots'), parts along dimension 0, may hold values from -48 to 48
- source_cell: int32 [2], P('shots'), parts along dimension 0, may hold values from 0 to 2097151
- receivers: int32 [2048], P('shots'), parts along dimension 0, may hold values from 0 to 2097151
- observed: float32 [24, 1024], P('shots'), parts along dimension 0, may hold values from -6 to 6
- footprint: int32 [4096], P(('shots', 'gx')), parts along dimension 0, may hold values 0 or 1
- brick_owner: int32 [2048, 1], P('gx'), may hold values from 0 to 15; in each aligned block of 128 rows (0 to 127, 128 to 255, ...) at most 16 rows name the same one
- prior_in: bfloat16 [32, 27], replicated, may hold values from -1.25 to 1.25
- prior_in_bias: float32 [32], replicated, may hold values from -3 to 3
- prior_mix: bfloat16 [32, 32], replicated, may hold values from -1 to 1
- prior_mix_bias: float32 [32], replicated, may hold values from -3 to 3
- prior_out: bfloat16 [27, 32], replicated, may hold values from -0.21875 to 0.21875
- prior_out_bias: float32 [1], replicated, may hold values from -3 to 3
Outputs:
- residual_traces: float32 [24, 1024], P('shots'), parts along dimension 0
- owned_bricks: bfloat16 [32, 16, 16, 1024], P(('shots', 'gx')), parts along dimension 0
There are 2 independent parts, one for each index of `shots`. A program takes and returns all parts, laid end to end along the dimension named above; an argument that names none is the same for every part. Nothing has to cross between parts.
Inputs may be any that keep to these rules, and one draw needn't show every extreme that they name: `brick_owner`: among the 128 bricks of one device's block, at most 16 have the same owner.
All inputs are finite; a program needn't handle non-finite values. No bound on the sum of `footprint` on one device may be relied on, other than what follows from the above.
Results may differ from a plain program's by a relative error of at most 0.0045.
Values may be sent and summed in bfloat16 or wider, within the bound.
A program may use at most 128 MiB of HBM per device.

v0:
```python
import jax
import jax.numpy as jnp
from jax import lax
from jax.sharding import PartitionSpec as P

OFFSETS = [(a, b, c) for a in range(3) for b in range(3) for c in range(3)]


def padded_2(cells, sides, width):
    for axis, dim in sides:
        count = lax.axis_size(axis)
        ends = count - 1
        head = lax.slice_in_dim(cells, 0, width, axis=dim)
        tail = lax.slice_in_dim(cells, cells.shape[dim] - width, cells.shape[dim], axis=dim)
        cells = jnp.concatenate(
            [
                lax.ppermute(tail, axis, [(i, (i + 1) % count) for i in range(ends)]),
                cells,
                lax.ppermute(head, axis, [((i + 1) % count, i) for i in range(ends)]),
            ],
            axis=dim,
        )
    return cells


def laplace(widened):
    inner = widened[2:-2]
    along_x = 16.0 * (widened[3:-1] + widened[1:-3]) - (widened[4:] + widened[:-4])
    pad_y = jnp.pad(inner, ((0, 0), (2, 2), (0, 0)))
    along_y = 16.0 * (pad_y[:, 3:-1] + pad_y[:, 1:-3]) - (pad_y[:, 4:] + pad_y[:, :-4])
    pad_z = jnp.pad(inner, ((0, 0), (0, 0), (2, 2)))
    along_z = 16.0 * (pad_z[:, :, 3:-1] + pad_z[:, :, 1:-3]) - (pad_z[:, :, 4:] + pad_z[:, :, :-4])
    return (along_x + along_y + along_z - 90.0 * inner) / 12.0


def leapfrog(before, widened, coeffs):
    return 2.0 * widened[2:-2] - before + coeffs * laplace(widened)


def inject(field, base_x, cells, values):
    plane = field.shape[1] * field.shape[2]
    count = field.shape[0] * plane
    relative = cells - base_x * plane
    inside = (relative >= 0) & (relative < count)
    clipped = jnp.clip(relative, 0, count - 1)
    flattened = field.reshape(-1).at[clipped].add(jnp.where(inside, values, 0.0))
    return flattened.reshape(field.shape)


def sample(field, base_x, cells):
    plane = field.shape[1] * field.shape[2]
    count = field.shape[0] * plane
    relative = cells - base_x * plane
    inside = (relative >= 0) & (relative < count)
    clipped = jnp.clip(relative, 0, count - 1)
    return jnp.where(inside, field.reshape(-1)[clipped], 0.0)


def lifting(widened, weight_in, bias_in, weight_mix, bias_mix):
    planes = widened.shape[0] - 2
    rows_y = widened.shape[1]
    rows_z = widened.shape[2]
    padded = jnp.pad(widened, ((0, 0), (1, 1), (1, 1)))
    stacked = jnp.stack(
        [padded[a : a + planes, b : b + rows_y, c : c + rows_z] for a, b, c in OFFSETS]
    ).reshape(27, -1)
    lifted = jnp.dot(weight_in, stacked, preferred_element_type=jnp.float32) + bias_in[:, None]
    lifted = jnp.maximum(lifted, 0.0).astype(jnp.bfloat16)
    hidden = jnp.dot(weight_mix, lifted, preferred_element_type=jnp.float32) + bias_mix[:, None]
    return jnp.maximum(hidden, 0.0).astype(jnp.bfloat16).reshape(-1, planes, rows_y, rows_z)


def project(widened, weight_out, bias_out):
    channels = widened.shape[0]
    planes = widened.shape[1] - 2
    rows_y = widened.shape[2]
    rows_z = widened.shape[3]
    products = jnp.dot(
        weight_out, widened.reshape(channels, -1), preferred_element_type=jnp.float32
    )
    products = jnp.pad(
        products.reshape(27, planes + 2, rows_y, rows_z), ((0, 0), (0, 0), (1, 1), (1, 1))
    )
    summed = jnp.zeros((planes, rows_y, rows_z), jnp.float32)
    for position, (a, b, c) in enumerate(OFFSETS):
        summed = summed + products[position, a : a + planes, b : b + rows_y, c : c + rows_z]
    return summed + bias_out[0]


def rim_one(field):
    return padded_2(field, (("gx", 0),), 2)


def per_device(
    courant_sq,
    wave_prev,
    wave_now,
    adj_late,
    adj_last,
    wavelet,
    source_cell,
    receivers,
    observed,
    footprint,
    brick_owner,
    prior_in,
    prior_in_bias,
    prior_mix,
    prior_mix_bias,
    prior_out,
    prior_out_bias,
):
    cells_x, cells_y, cells_z = wave_now.shape
    devices = lax.axis_size("gx")
    anchor = lax.axis_index("gx") * cells_x
    total_x = cells_x * devices
    field_shape = wave_now.shape

    def forward_step(loop_state, impulse):
        before, current = loop_state
        newest = inject(
            leapfrog(before, rim_one(current), courant_sq), anchor, source_cell, impulse[None]
        )
        return (
            (current, newest),
            (newest - 2.0 * current + before, sample(newest, anchor, receivers)),
        )

    _, (changes, records) = lax.scan(forward_step, (wave_prev, wave_now), wavelet)
    residual_traces = lax.psum(records, "gx") - observed
    zeros_field = jnp.zeros(field_shape, jnp.float32)

    def adjoint_step(loop_state, inputs):
        future, current, summed = loop_state
        misfit, change = inputs
        newest = inject(leapfrog(future, rim_one(current), courant_sq), anchor, receivers, misfit)
        return ((current, newest, summed + newest * change), None)

    (_, _, grad), _ = lax.scan(
        adjoint_step, (adj_late, adj_last, zeros_field), (residual_traces[::-1], changes[::-1])
    )
    grad_low = grad.astype(jnp.bfloat16)
    grad_wide = padded_2(grad_low, (("gx", 0),), 2)
    hidden = lifting(grad_wide, prior_in, prior_in_bias, prior_mix, prior_mix_bias)
    margin = anchor - 1 + jnp.arange(cells_x + 2, dtype=jnp.int32)
    keep = ((margin >= 0) & (margin < total_x))[None, :, None, None]
    hidden_wide = jnp.where(keep, hidden, jnp.zeros_like(hidden))
    conv = project(hidden_wide, prior_out, prior_out_bias)
    model_grad = (grad + conv).astype(jnp.bfloat16)
    bricks = model_grad.transpose(1, 0, 2).reshape(cells_y, cells_x * cells_z)
    bricks = jnp.where((footprint == 1)[:, None], bricks, jnp.zeros_like(bricks))
    owners = brick_owner[:, 0]
    same = owners[:, None] == owners[None, :]
    lower = (
        jnp.arange(cells_y, dtype=jnp.int32)[:, None]
        > jnp.arange(cells_y, dtype=jnp.int32)[None, :]
    )
    slots = jnp.sum((same & lower).astype(jnp.int32), axis=1)
    capacity = max(2, 2 * cells_y // devices)
    buckets = (
        jnp.zeros((devices, capacity, cells_x * cells_z), jnp.bfloat16)
        .at[owners, slots]
        .set(bricks)
    )
    arrived = lax.all_to_all(buckets, "gx", split_axis=0, concat_axis=0, tiled=True)
    return (residual_traces, arrived[None])


def solution(mesh):
    return jax.shard_map(
        per_device,
        mesh=mesh,
        in_specs=(
            P("gx", None, None),
            P(("shots", "gx"), None, None),
            P(("shots", "gx"), None, None),
            P(("shots", "gx"), None, None),
            P(("shots", "gx"), None, None),
            P("shots"),
            P("shots"),
            P("shots"),
            P("shots", None),
            P(("shots", "gx")),
            P("gx", None),
            P(),
            P(),
            P(),
            P(),
            P(),
            P(),
        ),
        out_specs=(P("shots", None), P(("shots", "gx"), None, None, None)),
        check_vma=False,
    )
```

profile of v0, /device:TPU:11, one launch (start us, length us, event | category | flops | bytes accessed | tf_op | source)
XLA Modules:
  0.0 700.3 jit_solution(2389430900600771791)
XLA Ops:
  3.5 228.7 %while.36 = (s32[]{:T(128)}, f32[8,128,128]{2,1,0:T(8,128)S(1)}, f32[8,128,128]{2,1,0:T(8,128)S(1)}, f32[12,8,128,128]{3,2,1,0:T(8,128)}, f32[12,1024]{1,0:T(8,1...) while((s32[]{:T(128)}, f32[8,128,128]{2,1,0:T(8,128)S(1)}, ...), condition=%wide.region_1.2_spmd, body=%wide.region_0.1_spmd.sunk | while | flops 3156997 | bytes 12133655 | solution.py:129
  232.2 45.2 %psum.7 = f32[12,1024]{1,0:T(8,128)S(1)} all-reduce(f32[12,1024]{1,0:T(8,128)S(1)} %get-tuple-element.278), channel_id=1, replica_groups=mesh['shots'=2,'gx'=16] {'gx'}, use_global_device_ids=true, to_apply=%region_2.3 | all-reduce | flops 12288 | bytes 98304 | tf_op jit(solution)/shard_map/psum | solution.py:130
  283.9 220.2 %while.37 = (s32[]{:T(128)}, f32[8,128,128]{2,1,0:T(8,128)S(1)}, f32[8,128,128]{2,1,0:T(8,128)S(1)}, f32[8,128,128]{2,1,0:T(8,128)S(1)}, f32[8,128,128]{2,1,0:T(...) while((s32[]{:T(128)}, f32[8,128,128]{2,1,0:T(8,128)S(1)}, ...), condition=%wide.region_6.7_spmd.clone, body=%wide.region_4.6_spmd.clone.sunk | while | flops 3156995 | bytes 12112095 | solution.py:139
  294.6 6.4 scatter_fusion
  312.3 6.4 scatter_fusion
  322.1 6.6 collective-permute-start.3
  330.4 6.4 scatter_fusion
  340.2 6.5 collective-permute-start.3
  348.5 6.4 scatter_fusion
  358.3 6.5 collective-permute-start.3
  369.0 6.4 scatter_fusion
  387.2 6.4 scatter_fusion
  405.4 6.4 scatter_fusion
  423.7 6.4 scatter_fusion
  441.9 6.4 scatter_fusion
  460.1 6.4 scatter_fusion
  478.2 6.4 scatter_fusion
  563.7 54.1 %stack.111 = bf16[27,163840]{1,0:T(8,128)(2,1)} concatenate(bf16[1,163840]{1,0:T(2,128)(2,1)} %stack.84, bf16[1,163840]{1,0:T(2,128)(2,1)} %stack.85, bf16[1,163840]{1,0:T(2,128)(2,1)} %stack.86, bf16[1,163840]{1,0:T(2,128)(2,1)} %stack.87, bf16[1,163840]{1,0:T(2,128)(2,1)S(1)} %stack.88, bf16[1,163840]{1,0:T(2,128)(2,1)} %stack.89, bf16[1,163840]{1,0:T(2,128)(2,1)} %stack.90, ...), dimensions={0} | concatenate | bytes 17694720 | tf_op jit(solution)/shard_map/stack | solution.py:64
  617.9 10.8 %fusion.31 = bf16[163840,32]{0,1:T(8,128)(2,1)} fusion(bf16[27,163840]{1,0:T(8,128)(2,1)} %stack.111, bf16[32,27]{1,0:T(8,128)(2,1)S(1)} %copy-done, f32[32]{0:T(128)S(1)} %copy-done.12), kind=kOutput, calls=%fused_computation.95 | convolution fusion | flops 298844160 | bytes 19334976 | tf_op jit(solution)/shard_map/dot_general | solution.py:67
  628.9 12.7 %fusion.35 = f32[163840,27]{0,1:T(8,128)} fusion(bf16[27,32]{1,0:T(8,128)(2,1)S(1)} %copy-done.10, bf16[32,32]{1,0:T(8,128)(2,1)S(1)} %copy-done.9, bf16[163840,32]{0,1:T(8,128)(2,1)} %fusion.31, f32[32]{0:T(128)S(1)} %copy-done.11, pred[163840]{0:T(1024)(128)(4,1)S(1)} %bitcast.208), kind=kOutput, calls=%fused_computation.99 | convolution fusion | flops 639631360 | bytes 28348224 | tf_op jit(solution)/shard_map/dot_general | solution.py:78
  641.6 19.2 %copy.23 = f32[4,8,1280,128]{3,2,1,0:T(8,128)} copy(f32[4,8,1280,128]{3,1,2,0:T(8,128)} %bitcast.204) | data formatting | bytes 41943040
  660.9 7.1 %slice.443 = f32[27,1280,128]{2,1,0:T(8,128)S(1)} slice(f32[32,1280,128]{2,1,0:T(8,128)} %bitcast.206), slice={[0:27], [0:1280], [0:128]} | slice | bytes 35389440
  670.5 9.0 %scatter_fusion.1 = bf16[16,16,1024]{2,1,0:T(8,128)(2,1)S(1)} fusion(bf16[16,16,1024]{2,1,0:T(8,128)(2,1)S(1)} %broadcast_in_dim.77, s32[128]{0:T(128)S(1)} %fusion.78, bf16[128,1024]{1,0:T(8,128)(2,1)S(1)} %bitcast_select_fusion), kind=kCustom, calls=%fused_computation.2 | custom fusion | bytes 787456 | tf_op jit(solution)/shard_map/scatter | solution.py:163
  679.5 20.0 %all_to_all.5 = bf16[16,16,1024]{2,1,0:T(8,128)(2,1)S(1)} all-to-all(bf16[16,16,1024]{2,1,0:T(8,128)(2,1)S(1)} %scatter_fusion.1), channel_id=1, replica_groups=mesh['shots'=2,'gx'=16] {'gx'}, dimensions={0} | all-to-all | bytes 1048576 | tf_op jit(solution)/shard_map/all_to_all | solution.py:165
  (523 shorter events, 426.5 us)
Async XLA Ops:
  44.2 7.2 %collective-permute-start.1 = (f32[2,128,128]{2,1,0:T(8,128)S(1)}, f32[2,128,128]{2,1,0:T(8,128)S(1)}, u32[]{:S(2)}, u32[]{:S(2)}) collective-permute-start(f32[2,128,128]{2,1,0:T(8,128)S(1)} %get-tuple-element.520), channel_id=1, source_target_pairs={{1,0},{2,1},{3,2},{4,3},{5,4},{6,5},{7,6},{8,7},{9,8},{10,9},{11,1... | collective-permute-start | bytes 393224 | tf_op jit(solution)/shard_map/while/body/eval_jaxpr/ppermute | solution.py:19
  63.2 7.2 %collective-permute-start.1 = (f32[2,128,128]{2,1,0:T(8,128)S(1)}, f32[2,128,128]{2,1,0:T(8,128)S(1)}, u32[]{:S(2)}, u32[]{:S(2)}) collective-permute-start(f32[2,128,128]{2,1,0:T(8,128)S(1)} %get-tuple-element.520), channel_id=1, source_target_pairs={{1,0},{2,1},{3,2},{4,3},{5,4},{6,5},{7,6},{8,7},{9,8},{10,9},{11,1... | collective-permute-start | bytes 393224 | tf_op jit(solution)/shard_map/while/body/eval_jaxpr/ppermute | solution.py:19
  82.2 7.2 %collective-permute-start.1 = (f32[2,128,128]{2,1,0:T(8,128)S(1)}, f32[2,128,128]{2,1,0:T(8,128)S(1)}, u32[]{:S(2)}, u32[]{:S(2)}) collective-permute-start(f32[2,128,128]{2,1,0:T(8,128)S(1)} %get-tuple-element.520), channel_id=1, source_target_pairs={{1,0},{2,1},{3,2},{4,3},{5,4},{6,5},{7,6},{8,7},{9,8},{10,9},{11,1... | collective-permute-start | bytes 393224 | tf_op jit(solution)/shard_map/while/body/eval_jaxpr/ppermute | solution.py:19
  101.2 7.2 %collective-permute-start.1 = (f32[2,128,128]{2,1,0:T(8,128)S(1)}, f32[2,128,128]{2,1,0:T(8,128)S(1)}, u32[]{:S(2)}, u32[]{:S(2)}) collective-permute-start(f32[2,128,128]{2,1,0:T(8,128)S(1)} %get-tuple-element.520), channel_id=1, source_target_pairs={{1,0},{2,1},{3,2},{4,3},{5,4},{6,5},{7,6},{8,7},{9,8},{10,9},{11,1... | collective-permute-start | bytes 393224 | tf_op jit(solution)/shard_map/while/body/eval_jaxpr/ppermute | solution.py:19
  120.2 7.2 %collective-permute-start.1 = (f32[2,128,128]{2,1,0:T(8,128)S(1)}, f32[2,128,128]{2,1,0:T(8,128)S(1)}, u32[]{:S(2)}, u32[]{:S(2)}) collective-permute-start(f32[2,128,128]{2,1,0:T(8,128)S(1)} %get-tuple-element.520), channel_id=1, source_target_pairs={{1,0},{2,1},{3,2},{4,3},{5,4},{6,5},{7,6},{8,7},{9,8},{10,9},{11,1... | collective-permute-start | bytes 393224 | tf_op jit(solution)/shard_map/while/body/eval_jaxpr/ppermute | solution.py:19
  139.2 7.2 %collective-permute-start.1 = (f32[2,128,128]{2,1,0:T(8,128)S(1)}, f32[2,128,128]{2,1,0:T(8,128)S(1)}, u32[]{:S(2)}, u32[]{:S(2)}) collective-permute-start(f32[2,128,128]{2,1,0:T(8,128)S(1)} %get-tuple-element.520), channel_id=1, source_target_pairs={{1,0},{2,1},{3,2},{4,3},{5,4},{6,5},{7,6},{8,7},{9,8},{10,9},{11,1... | collective-permute-start | bytes 393224 | tf_op jit(solution)/shard_map/while/body/eval_jaxpr/ppermute | solution.py:19
  158.2 7.2 %collective-permute-start.1 = (f32[2,128,128]{2,1,0:T(8,128)S(1)}, f32[2,128,128]{2,1,0:T(8,128)S(1)}, u32[]{:S(2)}, u32[]{:S(2)}) collective-permute-start(f32[2,128,128]{2,1,0:T(8,128)S(1)} %get-tuple-element.520), channel_id=1, source_target_pairs={{1,0},{2,1},{3,2},{4,3},{5,4},{6,5},{7,6},{8,7},{9,8},{10,9},{11,1... | collective-permute-start | bytes 393224 | tf_op jit(solution)/shard_map/while/body/eval_jaxpr/ppermute | solution.py:19
  177.2 7.2 %collective-permute-start.1 = (f32[2,128,128]{2,1,0:T(8,128)S(1)}, f32[2,128,128]{2,1,0:T(8,128)S(1)}, u32[]{:S(2)}, u32[]{:S(2)}) collective-permute-start(f32[2,128,128]{2,1,0:T(8,128)S(1)} %get-tuple-element.520), channel_id=1, source_target_pairs={{1,0},{2,1},{3,2},{4,3},{5,4},{6,5},{7,6},{8,7},{9,8},{10,9},{11,1... | collective-permute-start | bytes 393224 | tf_op jit(solution)/shard_map/while/body/eval_jaxpr/ppermute | solution.py:19
  215.1 7.2 %collective-permute-start.1 = (f32[2,128,128]{2,1,0:T(8,128)S(1)}, f32[2,128,128]{2,1,0:T(8,128)S(1)}, u32[]{:S(2)}, u32[]{:S(2)}) collective-permute-start(f32[2,128,128]{2,1,0:T(8,128)S(1)} %get-tuple-element.520), channel_id=1, source_target_pairs={{1,0},{2,1},{3,2},{4,3},{5,4},{6,5},{7,6},{8,7},{9,8},{10,9},{11,1... | collective-permute-start | bytes 393224 | tf_op jit(solution)/shard_map/while/body/eval_jaxpr/ppermute | solution.py:19
  284.0 9.0 %collective-permute-start.2 = (f32[2,128,128]{2,1,0:T(8,128)S(1)}, f32[2,128,128]{2,1,0:T(8,128)S(1)}, u32[]{:S(2)}, u32[]{:S(2)}) collective-permute-start(f32[2,128,128]{2,1,0:T(8,128)S(1)} %get-tuple-element.530), channel_id=1, source_target_pairs={{0,1},{1,2},{2,3},{3,4},{4,5},{5,6},{6,7},{7,8},{8,9},{9,10},{10,1... | collective-permute-start | bytes 393224 | tf_op jit(solution)/shard_map/while/body/eval_jaxpr/ppermute | solution.py:17
  302.5 8.1 %collective-permute-start.2 = (f32[2,128,128]{2,1,0:T(8,128)S(1)}, f32[2,128,128]{2,1,0:T(8,128)S(1)}, u32[]{:S(2)}, u32[]{:S(2)}) collective-permute-start(f32[2,128,128]{2,1,0:T(8,128)S(1)} %get-tuple-element.530), channel_id=1, source_target_pairs={{0,1},{1,2},{2,3},{3,4},{4,5},{5,6},{6,7},{7,8},{8,9},{9,10},{10,1... | collective-permute-start | bytes 393224 | tf_op jit(solution)/shard_map/while/body/eval_jaxpr/ppermute | solution.py:17
  320.1 8.6 %collective-permute-start.2 = (f32[2,128,128]{2,1,0:T(8,128)S(1)}, f32[2,128,128]{2,1,0:T(8,128)S(1)}, u32[]{:S(2)}, u32[]{:S(2)}) collective-permute-start(f32[2,128,128]{2,1,0:T(8,128)S(1)} %get-tuple-element.530), channel_id=1, source_target_pairs={{0,1},{1,2},{2,3},{3,4},{4,5},{5,6},{6,7},{7,8},{8,9},{9,10},{10,1... | collective-permute-start | bytes 393224 | tf_op jit(solution)/shard_map/while/body/eval_jaxpr/ppermute | solution.py:17
  322.1 7.6 %collective-permute-start.3 = (f32[2,128,128]{2,1,0:T(8,128)S(1)}, f32[2,128,128]{2,1,0:T(8,128)S(1)}, u32[]{:S(2)}, u32[]{:S(2)}) collective-permute-start(f32[2,128,128]{2,1,0:T(8,128)S(1)} %get-tuple-element.533), channel_id=1, source_target_pairs={{1,0},{2,1},{3,2},{4,3},{5,4},{6,5},{7,6},{8,7},{9,8},{10,9},{11,1... | collective-permute-start | bytes 393224 | tf_op jit(solution)/shard_map/while/body/eval_jaxpr/ppermute | solution.py:19
  338.3 8.5 %collective-permute-start.2 = (f32[2,128,128]{2,1,0:T(8,128)S(1)}, f32[2,128,128]{2,1,0:T(8,128)S(1)}, u32[]{:S(2)}, u32[]{:S(2)}) collective-permute-start(f32[2,128,128]{2,1,0:T(8,128)S(1)} %get-tuple-element.530), channel_id=1, source_target_pairs={{0,1},{1,2},{2,3},{3,4},{4,5},{5,6},{6,7},{7,8},{8,9},{9,10},{10,1... | collective-permute-start | bytes 393224 | tf_op jit(solution)/shard_map/while/body/eval_jaxpr/ppermute | solution.py:17
  340.2 7.5 %collective-permute-start.3 = (f32[2,128,128]{2,1,0:T(8,128)S(1)}, f32[2,128,128]{2,1,0:T(8,128)S(1)}, u32[]{:S(2)}, u32[]{:S(2)}) collective-permute-start(f32[2,128,128]{2,1,0:T(8,128)S(1)} %get-tuple-element.533), channel_id=1, source_target_pairs={{1,0},{2,1},{3,2},{4,3},{5,4},{6,5},{7,6},{8,7},{9,8},{10,9},{11,1... | collective-permute-start | bytes 393224 | tf_op jit(solution)/shard_map/while/body/eval_jaxpr/ppermute | solution.py:19
  356.3 8.5 %collective-permute-start.2 = (f32[2,128,128]{2,1,0:T(8,128)S(1)}, f32[2,128,128]{2,1,0:T(8,128)S(1)}, u32[]{:S(2)}, u32[]{:S(2)}) collective-permute-start(f32[2,128,128]{2,1,0:T(8,128)S(1)} %get-tuple-element.530), channel_id=1, source_target_pairs={{0,1},{1,2},{2,3},{3,4},{4,5},{5,6},{6,7},{7,8},{8,9},{9,10},{10,1... | collective-permute-start | bytes 393224 | tf_op jit(solution)/shard_map/while/body/eval_jaxpr/ppermute | solution.py:17
  358.3 10.0 %collective-permute-start.3 = (f32[2,128,128]{2,1,0:T(8,128)S(1)}, f32[2,128,128]{2,1,0:T(8,128)S(1)}, u32[]{:S(2)}, u32[]{:S(2)}) collective-permute-start(f32[2,128,128]{2,1,0:T(8,128)S(1)} %get-tuple-element.533), channel_id=1, source_target_pairs={{1,0},{2,1},{3,2},{4,3},{5,4},{6,5},{7,6},{8,7},{9,8},{10,9},{11,1... | collective-permute-start | bytes 393224 | tf_op jit(solution)/shard_map/while/body/eval_jaxpr/ppermute | solution.py:19
  378.8 7.7 %collective-permute-start.3 = (f32[2,128,128]{2,1,0:T(8,128)S(1)}, f32[2,128,128]{2,1,0:T(8,128)S(1)}, u32[]{:S(2)}, u32[]{:S(2)}) collective-permute-start(f32[2,128,128]{2,1,0:T(8,128)S(1)} %get-tuple-element.533), channel_id=1, source_target_pairs={{1,0},{2,1},{3,2},{4,3},{5,4},{6,5},{7,6},{8,7},{9,8},{10,9},{11,1... | collective-permute-start | bytes 393224 | tf_op jit(solution)/shard_map/while/body/eval_jaxpr/ppermute | solution.py:19
  397.0 7.7 %collective-permute-start.3 = (f32[2,128,128]{2,1,0:T(8,128)S(1)}, f32[2,128,128]{2,1,0:T(8,128)S(1)}, u32[]{:S(2)}, u32[]{:S(2)}) collective-permute-start(f32[2,128,128]{2,1,0:T(8,128)S(1)} %get-tuple-element.533), channel_id=1, source_target_pairs={{1,0},{2,1},{3,2},{4,3},{5,4},{6,5},{7,6},{8,7},{9,8},{10,9},{11,1... | collective-permute-start | bytes 393224 | tf_op jit(solution)/shard_map/while/body/eval_jaxpr/ppermute | solution.py:19
  415.2 7.7 %collective-permute-start.3 = (f32[2,128,128]{2,1,0:T(8,128)S(1)}, f32[2,128,128]{2,1,0:T(8,128)S(1)}, u32[]{:S(2)}, u32[]{:S(2)}) collective-permute-start(f32[2,128,128]{2,1,0:T(8,128)S(1)} %get-tuple-element.533), channel_id=1, source_target_pairs={{1,0},{2,1},{3,2},{4,3},{5,4},{6,5},{7,6},{8,7},{9,8},{10,9},{11,1... | collective-permute-start | bytes 393224 | tf_op jit(solution)/shard_map/while/body/eval_jaxpr/ppermute | solution.py:19
  433.5 7.7 %collective-permute-start.3 = (f32[2,128,128]{2,1,0:T(8,128)S(1)}, f32[2,128,128]{2,1,0:T(8,128)S(1)}, u32[]{:S(2)}, u32[]{:S(2)}) collective-permute-start(f32[2,128,128]{2,1,0:T(8,128)S(1)} %get-tuple-element.533), channel_id=1, source_target_pairs={{1,0},{2,1},{3,2},{4,3},{5,4},{6,5},{7,6},{8,7},{9,8},{10,9},{11,1... | collective-permute-start | bytes 393224 | tf_op jit(solution)/shard_map/while/body/eval_jaxpr/ppermute | solution.py:19
  451.7 7.7 %collective-permute-start.3 = (f32[2,128,128]{2,1,0:T(8,128)S(1)}, f32[2,128,128]{2,1,0:T(8,128)S(1)}, u32[]{:S(2)}, u32[]{:S(2)}) collective-permute-start(f32[2,128,128]{2,1,0:T(8,128)S(1)} %get-tuple-element.533), channel_id=1, source_target_pairs={{1,0},{2,1},{3,2},{4,3},{5,4},{6,5},{7,6},{8,7},{9,8},{10,9},{11,1... | collective-permute-start | bytes 393224 | tf_op jit(solution)/shard_map/while/body/eval_jaxpr/ppermute | solution.py:19
  469.9 7.6 %collective-permute-start.3 = (f32[2,128,128]{2,1,0:T(8,128)S(1)}, f32[2,128,128]{2,1,0:T(8,128)S(1)}, u32[]{:S(2)}, u32[]{:S(2)}) collective-permute-start(f32[2,128,128]{2,1,0:T(8,128)S(1)} %get-tuple-element.533), channel_id=1, source_target_pairs={{1,0},{2,1},{3,2},{4,3},{5,4},{6,5},{7,6},{8,7},{9,8},{10,9},{11,1... | collective-permute-start | bytes 393224 | tf_op jit(solution)/shard_map/while/body/eval_jaxpr/ppermute | solution.py:19
  488.0 7.5 %collective-permute-start.3 = (f32[2,128,128]{2,1,0:T(8,128)S(1)}, f32[2,128,128]{2,1,0:T(8,128)S(1)}, u32[]{:S(2)}, u32[]{:S(2)}) collective-permute-start(f32[2,128,128]{2,1,0:T(8,128)S(1)} %get-tuple-element.533), channel_id=1, source_target_pairs={{1,0},{2,1},{3,2},{4,3},{5,4},{6,5},{7,6},{8,7},{9,8},{10,9},{11,1... | collective-permute-start | bytes 393224 | tf_op jit(solution)/shard_map/while/body/eval_jaxpr/ppermute | solution.py:19
  (52 other events, 2038.3 us)
where the time goes:
time: 710 us; the launch traced here: 700 us
  local copies, waits for them, and re-layouts  231 us (33%)
  other arithmetic  154 us (22%)
  starting transfers between devices  139 us (20%)
  waiting for transfers between devices  82.2 us (12%)
  blocking collectives  65.1 us (9%)
  matrix products  23.5 us (3%)
    another operation x28, local copies, waits for them, and re-layouts, lifting(): jnp.stack([padded[a:a + planes, b:b + rows_y, c:c + rows_z] for a, b, c i...  100 us
    ppermute x25, starting transfers between devices, padded_2(): lax.ppermute(head, axis, [((i + 1) % count, i) for i in range(ends)])  87.4 us
    scatter-add x24, other arithmetic, inject(): field.reshape(-1).at[clipped].add(jnp.where(inside, values, 0.0))  87.1 us
    ppermute x25, waiting for transfers between devices, padded_2(): lax.ppermute(head, axis, [((i + 1) % count, i) for i in range(ends)])  82.1 us
    gather x12, local copies, waits for them, and re-layouts, sample(): return jnp.where(inside, field.reshape(-1)[clipped], 0.0)  73.7 us
    ppermute x25, starting transfers between devices, padded_2(): lax.ppermute(tail, axis, [(i, (i + 1) % count) for i in range(ends)])  51.5 us
    psum x1, blocking collectives, per_device(): residual_traces = lax.psum(records, 'gx') - observed  45.2 us
    unnamed x33, local copies, waits for them, and re-layouts  29.3 us
  transfers between devices with their start and end apart: 50, of which 25 were waited for; matrix products, arithmetic and copies ran while one was open for 2% of the time, Pallas kernels for 0%

commit v1 on v0

--- a/solution.py
+++ b/solution.py
@@ -2,8 +2,14 @@
 import jax.numpy as jnp
 from jax import lax
 from jax.sharding import PartitionSpec as P
+from jax.lax import all_gather
 
 OFFSETS = [(a, b, c) for a in range(3) for b in range(3) for c in range(3)]
+
+
+def follow_view(load, row_axis):
+    low = all_gather(load, row_axis).sum(axis=0)
+    return low
 
 
 def padded_2(cells, sides, width):
@@ -127,7 +133,7 @@
         )
 
     _, (changes, records) = lax.scan(forward_step, (wave_prev, wave_now), wavelet)
-    residual_traces = lax.psum(records, "gx") - observed
+    residual_traces = follow_view(records, "gx") - observed
     zeros_field = jnp.zeros(field_shape, jnp.float32)
 
     def adjoint_step(loop_state, inputs):

time: 710 us -> 683 us (0.962)
  blocking collectives: 65.1 us -> 41.9 us
  starting transfers between devices: 139 us -> 117 us
  waiting for transfers between devices: 82.2 us -> 99 us
    psum x1 -> x0, blocking collectives: 45.2 us -> none  [per_device(): residual_traces = lax.psum(records, 'gx') - observed]
    all_gather x0 -> x1, blocking collectives: none -> 21.9 us  [follow_view(): low = all_gather(load, row_axis).sum(axis=0)]
    ppermute x25, starting transfers between devices: 87.4 us -> 66.7 us  [padded_2(): lax.ppermute(head, axis, [((i + 1) % count, i) for i in range(ends)])]
    ppermute x25, waiting for transfers between devices: 82.1 us -> 98.9 us  [padded_2(): lax.ppermute(head, axis, [((i + 1) % count, i) for i in range(ends)])]
where the time goes in v1:
time: 683 us; the launch traced here: 673 us
  local copies, waits for them, and re-layouts  231 us (34%)
  other arithmetic  156 us (23%)
  starting transfers between devices  117 us (17%)
  waiting for transfers between devices  99 us (14%)
  blocking collectives  41.9 us (6%)
  matrix products  23.5 us (3%)
    another operation x28, local copies, waits for them, and re-layouts, lifting(): jnp.stack([padded[a:a + planes, b:b + rows_y, c:c + rows_z] for a, b, c i...  100 us
    ppermute x25, waiting for transfers between devices, padded_2(): lax.ppermute(head, axis, [((i + 1) % count, i) for i in range(ends)])  98.9 us
    scatter-add x24, other arithmetic, inject(): field.reshape(-1).at[clipped].add(jnp.where(inside, values, 0.0))  87.1 us
    gather x12, local copies, waits for them, and re-layouts, sample(): return jnp.where(inside, field.reshape(-1)[clipped], 0.0)  73.7 us
    ppermute x25, starting transfers between devices, padded_2(): lax.ppermute(head, axis, [((i + 1) % count, i) for i in range(ends)])  66.7 us
    ppermute x25, starting transfers between devices, padded_2(): lax.ppermute(tail, axis, [(i, (i + 1) % count) for i in range(ends)])  50.4 us
    unnamed x33, local copies, waits for them, and re-layouts  29.3 us
    add x24, other arithmetic, leapfrog(): return 2.0 * widened[2:-2] - before + coeffs * laplace(widened)  28.2 us
  transfers between devices with their start and end apart: 50, of which 25 were waited for; matrix products, arithmetic and copies ran while one was open for 2% of the time, Pallas kernels for 0%

profile of v1, /device:TPU:11, one launch (start us, length us, event | category | flops | bytes accessed | tf_op | source)
XLA Modules:
  0.0 673.3 jit_solution(1738072544071825721)
XLA Ops:
  3.5 228.7 %while.36 = (s32[]{:T(128)}, f32[8,128,128]{2,1,0:T(8,128)S(1)}, f32[8,128,128]{2,1,0:T(8,128)S(1)}, f32[12,8,128,128]{3,2,1,0:T(8,128)}, f32[12,1024]{1,0:T(8,1...) while((s32[]{:T(128)}, f32[8,128,128]{2,1,0:T(8,128)S(1)}, ...), condition=%wide.region_1.2_spmd, body=%wide.region_0.1_spmd.sunk | while | flops 3156997 | bytes 12133655 | solution.py:135
  34.9 6.1 gather_fusion
  232.2 21.9 %all-gather.1 = f32[16,12,1024]{2,1,0:T(8,128)} all-gather(f32[1,12,1024]{2,1,0:T(8,128)S(1)} %bitcast.216), channel_id=2, replica_groups=mesh['shots'=2,'gx'=16] {'gx'}, dimensions={0}, use_global_device_ids=true | all-gather | bytes 835584 | tf_op jit(solution)/shard_map/all_gather | solution.py:11
  255.7 6.2 rev.7
  262.0 215.1 %while.37 = (s32[]{:T(128)}, f32[8,128,128]{2,1,0:T(8,128)S(1)}, f32[8,128,128]{2,1,0:T(8,128)S(1)}, f32[8,128,128]{2,1,0:T(8,128)S(1)}, f32[8,128,128]{2,1,0:T(...) while((s32[]{:T(128)}, f32[8,128,128]{2,1,0:T(8,128)S(1)}, ...), condition=%wide.region_6.7_spmd.clone, body=%wide.region_4.6_spmd.clone.sunk | while | flops 3156995 | bytes 12112095 | solution.py:145
  271.5 6.4 scatter_fusion
  288.9 6.4 scatter_fusion
  306.9 6.4 scatter_fusion
  324.9 6.4 scatter_fusion
  343.0 6.4 scatter_fusion
  361.0 6.4 scatter_fusion
  379.1 6.4 scatter_fusion
  397.1 6.4 scatter_fusion
  415.2 6.4 scatter_fusion
  433.2 6.4 scatter_fusion
  451.2 6.4 scatter_fusion
  469.3 6.4 scatter_fusion
  536.8 54.1 %stack.111 = bf16[27,163840]{1,0:T(8,128)(2,1)} concatenate(bf16[1,163840]{1,0:T(2,128)(2,1)} %stack.84, bf16[1,163840]{1,0:T(2,128)(2,1)} %stack.85, bf16[1,163840]{1,0:T(2,128)(2,1)} %stack.86, bf16[1,163840]{1,0:T(2,128)(2,1)} %stack.87, bf16[1,163840]{1,0:T(2,128)(2,1)S(1)} %stack.88, bf16[1,163840]{1,0:T(2,128)(2,1)} %stack.89, bf16[1,163840]{1,0:T(2,128)(2,1)} %stack.90, ...), dimensions={0} | concatenate | bytes 17694720 | tf_op jit(solution)/shard_map/stack | solution.py:70
  590.9 10.8 %fusion.31 = bf16[163840,32]{0,1:T(8,128)(2,1)} fusion(bf16[27,163840]{1,0:T(8,128)(2,1)} %stack.111, bf16[32,27]{1,0:T(8,128)(2,1)S(1)} %copy-done, f32[32]{0:T(128)S(1)} %copy-done.12), kind=kOutput, calls=%fused_computation.95 | convolution fusion | flops 298844160 | bytes 19334976 | tf_op jit(solution)/shard_map/dot_general | solution.py:73
  601.9 12.7 %fusion.35 = f32[163840,27]{0,1:T(8,128)} fusion(bf16[27,32]{1,0:T(8,128)(2,1)S(1)} %copy-done.10, bf16[32,32]{1,0:T(8,128)(2,1)S(1)} %copy-done.9, bf16[163840,32]{0,1:T(8,128)(2,1)} %fusion.31, f32[32]{0:T(128)S(1)} %copy-done.11, pred[163840]{0:T(1024)(128)(4,1)S(1)} %bitcast.209), kind=kOutput, calls=%fused_computation.99 | convolution fusion | flops 639631360 | bytes 28348224 | tf_op jit(solution)/shard_map/dot_general | solution.py:84
  614.6 19.2 %copy.24 = f32[4,8,1280,128]{3,2,1,0:T(8,128)} copy(f32[4,8,1280,128]{3,1,2,0:T(8,128)} %bitcast.205) | data formatting | bytes 41943040
  633.9 7.1 %slice.443 = f32[27,1280,128]{2,1,0:T(8,128)S(1)} slice(f32[32,1280,128]{2,1,0:T(8,128)} %bitcast.207), slice={[0:27], [0:1280], [0:128]} | slice | bytes 35389440
  643.6 9.0 %scatter_fusion.1 = bf16[16,16,1024]{2,1,0:T(8,128)(2,1)S(1)} fusion(bf16[16,16,1024]{2,1,0:T(8,128)(2,1)S(1)} %broadcast_in_dim.77, s32[128]{0:T(128)S(1)} %fusion.78, bf16[128,1024]{1,0:T(8,128)(2,1)S(1)} %bitcast_select_fusion), kind=kCustom, calls=%fused_computation.2 | custom fusion | bytes 787456 | tf_op jit(solution)/shard_map/scatter | solution.py:169
  652.5 20.0 %all_to_all.5 = bf16[16,16,1024]{2,1,0:T(8,128)(2,1)S(1)} all-to-all(bf16[16,16,1024]{2,1,0:T(8,128)(2,1)S(1)} %scatter_fusion.1), channel_id=1, replica_groups=mesh['shots'=2,'gx'=16] {'gx'}, dimensions={0} | all-to-all | bytes 1048576 | tf_op jit(solution)/shard_map/all_to_all | solution.py:171
  (524 shorter events, 423.7 us)
Async XLA Ops:
  3.5 6.4 collective-permute-start
  7.2 6.3 collective-permute-start.1
  25.3 7.1 %collective-permute-start.1 = (f32[2,128,128]{2,1,0:T(8,128)S(1)}, f32[2,128,128]{2,1,0:T(8,128)S(1)}, u32[]{:S(2)}, u32[]{:S(2)}) collective-permute-start(f32[2,128,128]{2,1,0:T(8,128)S(1)} %get-tuple-element.520), channel_id=1, source_target_pairs={{1,0},{2,1},{3,2},{4,3},{5,4},{6,5},{7,6},{8,7},{9,8},{10,9},{11,1... | collective-permute-start | bytes 393224 | tf_op jit(solution)/shard_map/while/body/eval_jaxpr/ppermute | solution.py:25
  44.2 7.2 %collective-permute-start.1 = (f32[2,128,128]{2,1,0:T(8,128)S(1)}, f32[2,128,128]{2,1,0:T(8,128)S(1)}, u32[]{:S(2)}, u32[]{:S(2)}) collective-permute-start(f32[2,128,128]{2,1,0:T(8,128)S(1)} %get-tuple-element.520), channel_id=1, source_target_pairs={{1,0},{2,1},{3,2},{4,3},{5,4},{6,5},{7,6},{8,7},{9,8},{10,9},{11,1... | collective-permute-start | bytes 393224 | tf_op jit(solution)/shard_map/while/body/eval_jaxpr/ppermute | solution.py:25
  63.2 7.2 %collective-permute-start.1 = (f32[2,128,128]{2,1,0:T(8,128)S(1)}, f32[2,128,128]{2,1,0:T(8,128)S(1)}, u32[]{:S(2)}, u32[]{:S(2)}) collective-permute-start(f32[2,128,128]{2,1,0:T(8,128)S(1)} %get-tuple-element.520), channel_id=1, source_target_pairs={{1,0},{2,1},{3,2},{4,3},{5,4},{6,5},{7,6},{8,7},{9,8},{10,9},{11,1... | collective-permute-start | bytes 393224 | tf_op jit(solution)/shard_map/while/body/eval_jaxpr/ppermute | solution.py:25
  82.2 7.2 %collective-permute-start.1 = (f32[2,128,128]{2,1,0:T(8,128)S(1)}, f32[2,128,128]{2,1,0:T(8,128)S(1)}, u32[]{:S(2)}, u32[]{:S(2)}) collective-permute-start(f32[2,128,128]{2,1,0:T(8,128)S(1)} %get-tuple-element.520), channel_id=1, source_target_pairs={{1,0},{2,1},{3,2},{4,3},{5,4},{6,5},{7,6},{8,7},{9,8},{10,9},{11,1... | collective-permute-start | bytes 393224 | tf_op jit(solution)/shard_map/while/body/eval_jaxpr/ppermute | solution.py:25
  101.2 7.2 %collective-permute-start.1 = (f32[2,128,128]{2,1,0:T(8,128)S(1)}, f32[2,128,128]{2,1,0:T(8,128)S(1)}, u32[]{:S(2)}, u32[]{:S(2)}) collective-permute-start(f32[2,128,128]{2,1,0:T(8,128)S(1)} %get-tuple-element.520), channel_id=1, source_target_pairs={{1,0},{2,1},{3,2},{4,3},{5,4},{6,5},{7,6},{8,7},{9,8},{10,9},{11,1... | collective-permute-start | bytes 393224 | tf_op jit(solution)/shard_map/while/body/eval_jaxpr/ppermute | solution.py:25
  120.2 7.2 %collective-permute-start.1 = (f32[2,128,128]{2,1,0:T(8,128)S(1)}, f32[2,128,128]{2,1,0:T(8,128)S(1)}, u32[]{:S(2)}, u32[]{:S(2)}) collective-permute-start(f32[2,128,128]{2,1,0:T(8,128)S(1)} %get-tuple-element.520), channel_id=1, source_target_pairs={{1,0},{2,1},{3,2},{4,3},{5,4},{6,5},{7,6},{8,7},{9,8},{10,9},{11,1... | collective-permute-start | bytes 393224 | tf_op jit(solution)/shard_map/while/body/eval_jaxpr/ppermute | solution.py:25
  139.2 7.2 %collective-permute-start.1 = (f32[2,128,128]{2,1,0:T(8,128)S(1)}, f32[2,128,128]{2,1,0:T(8,128)S(1)}, u32[]{:S(2)}, u32[]{:S(2)}) collective-permute-start(f32[2,128,128]{2,1,0:T(8,128)S(1)} %get-tuple-element.520), channel_id=1, source_target_pairs={{1,0},{2,1},{3,2},{4,3},{5,4},{6,5},{7,6},{8,7},{9,8},{10,9},{11,1... | collective-permute-start | bytes 393224 | tf_op jit(solution)/shard_map/while/body/eval_jaxpr/ppermute | solution.py:25
  158.2 7.2 %collective-permute-start.1 = (f32[2,128,128]{2,1,0:T(8,128)S(1)}, f32[2,128,128]{2,1,0:T(8,128)S(1)}, u32[]{:S(2)}, u32[]{:S(2)}) collective-permute-start(f32[2,128,128]{2,1,0:T(8,128)S(1)} %get-tuple-element.520), channel_id=1, source_target_pairs={{1,0},{2,1},{3,2},{4,3},{5,4},{6,5},{7,6},{8,7},{9,8},{10,9},{11,1... | collective-permute-start | bytes 393224 | tf_op jit(solution)/shard_map/while/body/eval_jaxpr/ppermute | solution.py:25
  177.2 7.2 %collective-permute-start.1 = (f32[2,128,128]{2,1,0:T(8,128)S(1)}, f32[2,128,128]{2,1,0:T(8,128)S(1)}, u32[]{:S(2)}, u32[]{:S(2)}) collective-permute-start(f32[2,128,128]{2,1,0:T(8,128)S(1)} %get-tuple-element.520), channel_id=1, source_target_pairs={{1,0},{2,1},{3,2},{4,3},{5,4},{6,5},{7,6},{8,7},{9,8},{10,9},{11,1... | collective-permute-start | bytes 393224 | tf_op jit(solution)/shard_map/while/body/eval_jaxpr/ppermute | solution.py:25
  196.2 7.2 %collective-permute-start.1 = (f32[2,128,128]{2,1,0:T(8,128)S(1)}, f32[2,128,128]{2,1,0:T(8,128)S(1)}, u32[]{:S(2)}, u32[]{:S(2)}) collective-permute-start(f32[2,128,128]{2,1,0:T(8,128)S(1)} %get-tuple-element.520), channel_id=1, source_target_pairs={{1,0},{2,1},{3,2},{4,3},{5,4},{6,5},{7,6},{8,7},{9,8},{10,9},{11,1... | collective-permute-start | bytes 393224 | tf_op jit(solution)/shard_map/while/body/eval_jaxpr/ppermute | solution.py:25
  215.1 7.2 %collective-permute-start.1 = (f32[2,128,128]{2,1,0:T(8,128)S(1)}, f32[2,128,128]{2,1,0:T(8,128)S(1)}, u32[]{:S(2)}, u32[]{:S(2)}) collective-permute-start(f32[2,128,128]{2,1,0:T(8,128)S(1)} %get-tuple-element.520), channel_id=1, source_target_pairs={{1,0},{2,1},{3,2},{4,3},{5,4},{6,5},{7,6},{8,7},{9,8},{10,9},{11,1... | collective-permute-start | bytes 393224 | tf_op jit(solution)/shard_map/while/body/eval_jaxpr/ppermute | solution.py:25
  281.3 6.8 %collective-permute-start.3 = (f32[2,128,128]{2,1,0:T(8,128)S(1)}, f32[2,128,128]{2,1,0:T(8,128)S(1)}, u32[]{:S(2)}, u32[]{:S(2)}) collective-permute-start(f32[2,128,128]{2,1,0:T(8,128)S(1)} %get-tuple-element.533), channel_id=1, source_target_pairs={{1,0},{2,1},{3,2},{4,3},{5,4},{6,5},{7,6},{8,7},{9,8},{10,9},{11,1... | collective-permute-start | bytes 393224 | tf_op jit(solution)/shard_map/while/body/eval_jaxpr/ppermute | solution.py:25
  298.7 7.5 %collective-permute-start.3 = (f32[2,128,128]{2,1,0:T(8,128)S(1)}, f32[2,128,128]{2,1,0:T(8,128)S(1)}, u32[]{:S(2)}, u32[]{:S(2)}) collective-permute-start(f32[2,128,128]{2,1,0:T(8,128)S(1)} %get-tuple-element.533), channel_id=1, source_target_pairs={{1,0},{2,1},{3,2},{4,3},{5,4},{6,5},{7,6},{8,7},{9,8},{10,9},{11,1... | collective-permute-start | bytes 393224 | tf_op jit(solution)/shard_map/while/body/eval_jaxpr/ppermute | solution.py:25
  316.7 7.5 %collective-permute-start.3 = (f32[2,128,128]{2,1,0:T(8,128)S(1)}, f32[2,128,128]{2,1,0:T(8,128)S(1)}, u32[]{:S(2)}, u32[]{:S(2)}) collective-permute-start(f32[2,128,128]{2,1,0:T(8,128)S(1)} %get-tuple-element.533), channel_id=1, source_target_pairs={{1,0},{2,1},{3,2},{4,3},{5,4},{6,5},{7,6},{8,7},{9,8},{10,9},{11,1... | collective-permute-start | bytes 393224 | tf_op jit(solution)/shard_map/while/body/eval_jaxpr/ppermute | solution.py:25
  334.7 7.5 %collective-permute-start.3 = (f32[2,128,128]{2,1,0:T(8,128)S(1)}, f32[2,128,128]{2,1,0:T(8,128)S(1)}, u32[]{:S(2)}, u32[]{:S(2)}) collective-permute-start(f32[2,128,128]{2,1,0:T(8,128)S(1)} %get-tuple-element.533), channel_id=1, source_target_pairs={{1,0},{2,1},{3,2},{4,3},{5,4},{6,5},{7,6},{8,7},{9,8},{10,9},{11,1... | collective-permute-start | bytes 393224 | tf_op jit(solution)/shard_map/while/body/eval_jaxpr/ppermute | solution.py:25
  352.8 7.5 %collective-permute-start.3 = (f32[2,128,128]{2,1,0:T(8,128)S(1)}, f32[2,128,128]{2,1,0:T(8,128)S(1)}, u32[]{:S(2)}, u32[]{:S(2)}) collective-permute-start(f32[2,128,128]{2,1,0:T(8,128)S(1)} %get-tuple-element.533), channel_id=1, source_target_pairs={{1,0},{2,1},{3,2},{4,3},{5,4},{6,5},{7,6},{8,7},{9,8},{10,9},{11,1... | collective-permute-start | bytes 393224 | tf_op jit(solution)/shard_map/while/body/eval_jaxpr/ppermute | solution.py:25
  370.8 7.5 %collective-permute-start.3 = (f32[2,128,128]{2,1,0:T(8,128)S(1)}, f32[2,128,128]{2,1,0:T(8,128)S(1)}, u32[]{:S(2)}, u32[]{:S(2)}) collective-permute-start(f32[2,128,128]{2,1,0:T(8,128)S(1)} %get-tuple-element.533), channel_id=1, source_target_pairs={{1,0},{2,1},{3,2},{4,3},{5,4},{6,5},{7,6},{8,7},{9,8},{10,9},{11,1... | collective-permute-start | bytes 393224 | tf_op jit(solution)/shard_map/while/body/eval_jaxpr/ppermute | solution.py:25
  388.9 7.5 %collective-permute-start.3 = (f32[2,128,128]{2,1,0:T(8,128)S(1)}, f32[2,128,128]{2,1,0:T(8,128)S(1)}, u32[]{:S(2)}, u32[]{:S(2)}) collective-permute-start(f32[2,128,128]{2,1,0:T(8,128)S(1)} %get-tuple-element.533), channel_id=1, source_target_pairs={{1,0},{2,1},{3,2},{4,3},{5,4},{6,5},{7,6},{8,7},{9,8},{10,9},{11,1... | collective-permute-start | bytes 393224 | tf_op jit(solution)/shard_map/while/body/eval_jaxpr/ppermute | solution.py:25
  406.9 7.5 %collective-permute-start.3 = (f32[2,128,128]{2,1,0:T(8,128)S(1)}, f32[2,128,128]{2,1,0:T(8,128)S(1)}, u32[]{:S(2)}, u32[]{:S(2)}) collective-permute-start(f32[2,128,128]{2,1,0:T(8,128)S(1)} %get-tuple-element.533), channel_id=1, source_target_pairs={{1,0},{2,1},{3,2},{4,3},{5,4},{6,5},{7,6},{8,7},{9,8},{10,9},{11,1... | collective-permute-start | bytes 393224 | tf_op jit(solution)/shard_map/while/body/eval_jaxpr/ppermute | solution.py:25
  425.0 7.5 %collective-permute-start.3 = (f32[2,128,128]{2,1,0:T(8,128)S(1)}, f32[2,128,128]{2,1,0:T(8,128)S(1)}, u32[]{:S(2)}, u32[]{:S(2)}) collective-permute-start(f32[2,128,128]{2,1,0:T(8,128)S(1)} %get-tuple-element.533), channel_id=1, source_target_pairs={{1,0},{2,1},{3,2},{4,3},{5,4},{6,5},{7,6},{8,7},{9,8},{10,9},{11,1... | collective-permute-start | bytes 393224 | tf_op jit(solution)/shard_map/while/body/eval_jaxpr/ppermute | solution.py:25
  443.0 7.5 %collective-permute-start.3 = (f32[2,128,128]{2,1,0:T(8,128)S(1)}, f32[2,128,128]{2,1,0:T(8,128)S(1)}, u32[]{:S(2)}, u32[]{:S(2)}) collective-permute-start(f32[2,128,128]{2,1,0:T(8,128)S(1)} %get-tuple-element.533), channel_id=1, source_target_pairs={{1,0},{2,1},{3,2},{4,3},{5,4},{6,5},{7,6},{8,7},{9,8},{10,9},{11,1... | collective-permute-start | bytes 393224 | tf_op jit(solution)/shard_map/while/body/eval_jaxpr/ppermute | solution.py:25
  461.1 7.5 %collective-permute-start.3 = (f32[2,128,128]{2,1,0:T(8,128)S(1)}, f32[2,128,128]{2,1,0:T(8,128)S(1)}, u32[]{:S(2)}, u32[]{:S(2)}) collective-permute-start(f32[2,128,128]{2,1,0:T(8,128)S(1)} %get-tuple-element.533), channel_id=1, source_target_pairs={{1,0},{2,1},{3,2},{4,3},{5,4},{6,5},{7,6},{8,7},{9,8},{10,9},{11,1... | collective-permute-start | bytes 393224 | tf_op jit(solution)/shard_map/while/body/eval_jaxpr/ppermute | solution.py:25
  (52 other events, 1878.5 us)
